TPU v7x, 512 devices: a whole 4x8x8 slice. The times are simulated.
512 devices in a mesh: span: 32 (over z, x), sub: 16 (over y, core).
Axes of the slice: x: 4, y: 8, z: 8, core: 2. Of those that a mesh axis runs over, the one named last changes fastest.
Arguments:
- stress: bfloat16 [512, 768, 128], P(('span', 'sub')), may hold values from -6 to 6
- history: float32 [8, 512, 768], P(None, ('span', 'sub')), may hold values from -6 to 6
- retard: float32 [8], replicated, may hold values from 0.3 to 30
- compliance: float32 [8], replicated, may hold values from 0.2 to 2
- micro: float32 [512, 768], P(('span', 'sub')), may hold values from 0.5 to 5
- lengths: int32 [512], P(('span', 'sub')), may hold values from 1 to 768, 131072 in all
- multiplier_index: int32 [512, 768], P(('span', 'sub')), may hold values from 0 to 131071, as said below
- dual_block: bfloat16 [512, 768, 768], P(('span', 'sub')), may hold values from -1 to 4, as said below
- corner_map: bfloat16 [512, 768, 128], P(('span', 'sub')), may hold values from -0.21875 to 0.21875
- coarse_stiffness_inverse: float32 [32, 128, 128], P('span'), may hold values from -1 to 4, as said below
Outputs:
- solution: float32 [131072, 128], P(('span', 'sub'))
- residual: float32 [131072, 128], P(('span', 'sub'))
Inputs may be any that keep to these rules, and one draw needn't show every extreme that they name: `multiplier_index`: each slot of a subdomain names a multiplier held by its own device or by the device of the same sub index in one of the two neighbouring spans; multipliers 0 and 131071 are named in every draw. `dual_block`: each block is symmetric with a diagonal between 1 and 4. `coarse_stiffness_inverse`: each span's matrix is symmetric with a diagonal between 1 and 4.
All inputs are finite; a program needn't handle non-finite values. No bound on the sum of `lengths` on one device may be relied on, other than what follows from the above.
Results may differ from a plain program's by a relative error of at most 0.024.
Values may be sent and summed in bfloat16 or wider, within the bound.
A program may use at most 64 MiB of HBM per device.

v0:
```python
import jax
import jax.numpy as jnp
from jax import lax
from jax.sharding import PartitionSpec as P

ITERS = 2


def from_behind(shard, axis, by):
    size = lax.axis_size(axis)
    pairs = [(i, i + by) for i in range(size) if 0 <= i + by < size]
    return lax.ppermute(shard, axis, pairs)


def padded(shard, sides, width):
    for axis, dim in sides:
        size, length = (lax.axis_size(axis), shard.shape[dim])
        up = [(i, (i + 1) % size) for i in range(size - 1)]
        down = [(j, i) for i, j in up]
        last = lax.slice_in_dim(shard, length - width, length, axis=dim)
        leading = lax.slice_in_dim(shard, 0, width, axis=dim)
        before = lax.ppermute(last, axis, up)
        after = lax.ppermute(leading, axis, down)
        shard = jnp.concatenate([before, shard, after], axis=dim)
    return shard


def column_sums(left, right):
    return jnp.sum(left * right, axis=0)


def on_device(
    stress,
    history,
    retard,
    compliance,
    micro,
    lengths,
    multiplier_index,
    dual_block,
    corner_map,
    coarse_stiffness_inverse,
):
    sub_count = dual_block.shape[0]
    width = dual_block.shape[1]
    loads = stress.shape[2]
    owned = sub_count * width // 3
    groups = lax.axis_size("sub")
    here = lax.axis_index("span")
    live = (jnp.arange(width)[None, :] < lengths[:, None]).astype(jnp.float32)
    owner_dev = multiplier_index // owned
    window_pos = ((owner_dev // groups - here + 1) * owned + multiplier_index % owned).reshape(-1)
    weight_k = 1.0 - jnp.exp(-1.0 / retard)
    creep = jnp.sum(weight_k * compliance)
    past = jnp.sum(weight_k[:, None, None] * history, axis=0)
    relaxed = micro / (1.0 + micro)
    load = (
        (creep + 0.5 * relaxed[:, :, None]) * stress.astype(jnp.float32) - past[:, :, None]
    ) * live[:, :, None]

    def assemble(local):
        window = (
            jnp.zeros((3 * owned, loads), jnp.float32).at[window_pos].add(local.reshape(-1, loads))
        )
        from_next = from_behind(window[:owned], "span", -1)
        from_prev = from_behind(window[2 * owned :], "span", 1)
        return window[owned : 2 * owned] + from_next + from_prev

    kernel = coarse_stiffness_inverse[0]
    rhs = assemble(load)
    solution = jnp.zeros_like(rhs)
    residual = rhs
    direction = rhs
    norm_now = lax.psum(column_sums(residual, residual), ("span", "sub"))
    for step in range(ITERS):
        narrow = direction.astype(jnp.bfloat16)
        apply_window = padded(narrow, (("span", 0),), owned)
        gathered = (
            apply_window[window_pos].reshape(sub_count, width, loads).astype(jnp.float32)
            * live[:, :, None]
        ).astype(jnp.bfloat16)
        apply_local = jnp.einsum(
            "smn,snr->smr", dual_block, gathered, preferred_element_type=jnp.float32
        )
        corner_part = jnp.einsum(
            "smc,smr->cr", corner_map, gathered, preferred_element_type=jnp.float32
        )
        corner_residual = lax.psum(corner_part.astype(jnp.bfloat16), "sub").astype(jnp.float32)
        corner_update = jnp.dot(kernel, corner_residual, precision=lax.Precision.HIGHEST)
        spread_corners = jnp.einsum(
            "smc,cr->smr",
            corner_map,
            corner_update.astype(jnp.bfloat16),
            preferred_element_type=jnp.float32,
        )
        image = assemble((apply_local + spread_corners) * live[:, :, None])
        curve = lax.psum(column_sums(direction, image), ("span", "sub"))
        alpha = norm_now / curve
        solution = solution + alpha * direction
        residual = residual - alpha * image
        norm_next = lax.psum(column_sums(residual, residual), ("span", "sub"))
        direction = residual + norm_next / norm_now * direction
        norm_now = norm_next
    return (solution, residual)


def solution(mesh):
    placed = (
        P(("span", "sub"), None, None),
        P(None, ("span", "sub"), None),
        P(),
        P(),
        P(("span", "sub"), None),
        P(("span", "sub")),
        P(("span", "sub"), None),
        P(("span", "sub"), None, None),
        P(("span", "sub"), None, None),
        P("span", None, None),
    )
    return jax.shard_map(
        on_device,
        mesh=mesh,
        in_specs=placed,
        out_specs=(P(("span", "sub"), None), P(("span", "sub"), None)),
        check_vma=False,
    )
```

profile of v0, /device:TPU:10, one launch (start us, length us, event | category | flops | bytes accessed | tf_op | source)
XLA Modules:
  0.0 476.3 jit_solution(13964561409451314039)
XLA Ops:
  5.6 6.9 %scatter_custom_fusion = f32[768,128]{1,0:T(8,128)S(1)} fusion(s32[768]{0:T(1024)S(1)} %fusion.43, bf16[1,768,128]{2,1,0:T(8,128)(2,1)} %param.10, f32[768]{0:T(1024)S(1)} %fusion.41, f32[768]{0:T(1024)S(1)} %multiply_reduce_fusion.4, f32[768]{0:T(1024)S(1)} %fusion.46, f32[]{:T(128)} %constant.45.clone.1), kind=kCustom, calls=%fused_computation.25 | custom fusion | flops 491520 | bytes 602116 | tf_op jit(solution)/shard_map/scatter-add | solution.py:63
  12.5 2.4 collective-permute-start
  15.0 3.4 collective-permute-start.1
  19.6 2.2 collective-permute-done.1
  21.9 2.1 collective-permute-start.3
  23.9 3.9 collective-permute-start.2
  28.2 1.9 collective-permute-done.2
  30.1 1.9 gather_fusion
  32.4 48.7 %psum.43 = bf16[128,128]{0,1:T(8,128)(2,1)S(1)} all-reduce(bf16[128,128]{0,1:T(8,128)(2,1)S(1)} %fusion.8), channel_id=1, replica_groups=mesh['span'=32,'sub'=16] {'sub'}, use_global_device_ids=true, to_apply=%region_5.6 | all-reduce | flops 16384 | bytes 65536 | tf_op jit(solution)/shard_map/psum | solution.py:88
  82.4 6.1 %scatter_custom_fusion.1 = f32[768,128]{1,0:T(8,128)S(1)} fusion(s32[768]{0:T(1024)S(1)} %fusion.43, f32[768,128]{1,0:T(8,128)S(1)} %copy.14, f32[]{:T(128)} %constant.45.clone.1), kind=kCustom, calls=%fused_computation.44 | custom fusion | flops 98304 | bytes 393220 | tf_op jit(solution)/shard_map/scatter-add | solution.py:63
  88.6 1.9 collective-permute-start.4
  90.5 3.9 collective-permute-start.5
  95.4 1.9 collective-permute-done.5
  97.4 108.1 %all-reduce = (f32[128]{0:T(128)S(1)}, f32[128]{0:T(128)S(1)}) all-reduce(f32[128]{0:T(128)S(1)} %get-tuple-element.3, f32[128]{0:T(128)S(1)} %get-tuple-element.2), channel_id=1, replica_groups=mesh['span'=32,'sub'=16] {'span','sub'}, use_global_device_ids=true, to_apply=%region_4.5 | all-reduce | flops 256 | bytes 2048 | tf_op jit(solution)/shard_map/psum | solution.py:74
  205.6 94.5 %psum.45 = f32[128]{0:T(128)S(1)} all-reduce(f32[128]{0:T(128)S(1)} %multiply_reduce_fusion.1), channel_id=1, replica_groups=mesh['span'=32,'sub'=16] {'span','sub'}, use_global_device_ids=true, to_apply=%region_10.11 | all-reduce | flops 128 | bytes 1024 | tf_op jit(solution)/shard_map/psum | solution.py:101
  300.2 2.8 collective-permute-start.7
  302.9 3.1 collective-permute-start.6
  306.3 2.8 collective-permute-done.6
  312.0 42.7 %psum.46 = bf16[128,128]{0,1:T(8,128)(2,1)S(1)} all-reduce(bf16[128,128]{0,1:T(8,128)(2,1)S(1)} %fusion.9), channel_id=1, replica_groups=mesh['span'=32,'sub'=16] {'sub'}, use_global_device_ids=true, to_apply=%region_11.12 | all-reduce | flops 16384 | bytes 65536 | tf_op jit(solution)/shard_map/psum | solution.py:88
  355.3 6.1 %scatter_custom_fusion.2 = f32[768,128]{1,0:T(8,128)S(1)} fusion(s32[768]{0:T(1024)S(1)} %fusion.43, f32[768,128]{1,0:T(8,128)S(1)} %copy.15, f32[]{:T(128)} %constant.45.clone.1), kind=kCustom, calls=%fused_computation.42 | custom fusion | flops 98304 | bytes 393220 | tf_op jit(solution)/shard_map/scatter-add | solution.py:63
  361.5 1.9 collective-permute-start.8
  363.4 3.9 collective-permute-start.9
  368.4 1.9 collective-permute-done.9
  370.3 105.2 %psum.47 = f32[128]{0:T(128)S(1)} all-reduce(f32[128]{0:T(128)S(1)} %multiply_reduce_fusion), channel_id=1, replica_groups=mesh['span'=32,'sub'=16] {'span','sub'}, use_global_device_ids=true, to_apply=%region_14.15 | all-reduce | flops 128 | bytes 1024 | tf_op jit(solution)/shard_map/psum | solution.py:97
  (42 shorter events, 14.2 us)
Async XLA Ops:
  0.6 80.5 %copy-start = (bf16[1,768,768]{2,1,0:T(8,128)(2,1)S(1)}, bf16[1,768,768]{2,1,0:T(8,128)(2,1)}, u32[]{:S(2)}) copy-start(bf16[1,768,768]{2,1,0:T(8,128)(2,1)} %param.17) | copy-start | bytes 3538948
  12.5 7.1 %collective-permute-start = (f32[256,128]{1,0:T(8,128)S(1)}, f32[256,128]{1,0:T(8,128)S(1)}, u32[]{:S(2)}, u32[]{:S(2)}) collective-permute-start(f32[256,128]{1,0:T(8,128)S(1)} %get-tuple-element.15), channel_id=1, source_target_pairs={{16,0},{32,16},{48,32},{64,48},{80,64},{96,80},{112,96},{128,112},... | collective-permute-start | bytes 393224 | tf_op jit(solution)/shard_map/ppermute | solution.py:12
  15.0 6.9 %collective-permute-start.1 = (f32[256,128]{1,0:T(8,128)S(1)}, f32[256,128]{1,0:T(8,128)S(1)}, u32[]{:S(2)}, u32[]{:S(2)}) collective-permute-start(f32[256,128]{1,0:T(8,128)S(1)} %get-tuple-element.16), channel_id=1, source_target_pairs={{0,16},{16,32},{32,48},{48,64},{64,80},{80,96},{96,112},{112,128},... | collective-permute-start | bytes 393224 | tf_op jit(solution)/shard_map/ppermute | solution.py:12
  21.9 10.1 %copy-start.1 = (bf16[1,768,128]{2,1,0:T(8,128)(2,1)S(1)}, bf16[1,768,128]{2,1,0:T(8,128)(2,1)}, u32[]{:S(2)}) copy-start(bf16[1,768,128]{2,1,0:T(8,128)(2,1)} %param.18) | copy-start | bytes 589828
  21.9 6.3 %collective-permute-start.3 = (bf16[256,128]{1,0:T(8,128)(2,1)S(1)}, bf16[256,128]{1,0:T(8,128)(2,1)S(1)}, u32[]{:S(2)}, u32[]{:S(2)}) collective-permute-start(bf16[256,128]{1,0:T(8,128)(2,1)S(1)} %get-tuple-element.7), channel_id=1, source_target_pairs={{16,0},{32,16},{48,32},{64,48},{80,64},{96,80},{112,96},{128,112},... | collective-permute-start | bytes 196616 | tf_op jit(solution)/shard_map/ppermute | solution.py:23
  23.9 6.2 %collective-permute-start.2 = (bf16[256,128]{1,0:T(8,128)(2,1)S(1)}, bf16[256,128]{1,0:T(8,128)(2,1)S(1)}, u32[]{:S(2)}, u32[]{:S(2)}) collective-permute-start(bf16[256,128]{1,0:T(8,128)(2,1)S(1)} %get-tuple-element.7), channel_id=1, source_target_pairs={{0,16},{16,32},{32,48},{48,64},{64,80},{80,96},{96,112},{112,128},... | collective-permute-start | bytes 196616 | tf_op jit(solution)/shard_map/ppermute | solution.py:22
  32.0 49.8 %copy-start.2 = (f32[1,128,128]{2,1,0:T(8,128)S(1)}, f32[1,128,128]{2,1,0:T(8,128)}, u32[]{:S(2)}) copy-start(f32[1,128,128]{2,1,0:T(8,128)} %param.19) | copy-start | bytes 196612
  88.6 6.9 %collective-permute-start.4 = (f32[256,128]{1,0:T(8,128)S(1)}, f32[256,128]{1,0:T(8,128)S(1)}, u32[]{:S(2)}, u32[]{:S(2)}) collective-permute-start(f32[256,128]{1,0:T(8,128)S(1)} %get-tuple-element.13), channel_id=1, source_target_pairs={{16,0},{32,16},{48,32},{64,48},{80,64},{96,80},{112,96},{128,112},... | collective-permute-start | bytes 393224 | tf_op jit(solution)/shard_map/ppermute | solution.py:12
  90.5 6.9 %collective-permute-start.5 = (f32[256,128]{1,0:T(8,128)S(1)}, f32[256,128]{1,0:T(8,128)S(1)}, u32[]{:S(2)}, u32[]{:S(2)}) collective-permute-start(f32[256,128]{1,0:T(8,128)S(1)} %get-tuple-element.14), channel_id=1, source_target_pairs={{0,16},{16,32},{32,48},{48,64},{64,80},{80,96},{96,112},{112,128},... | collective-permute-start | bytes 393224 | tf_op jit(solution)/shard_map/ppermute | solution.py:12
  300.2 6.2 %collective-permute-start.7 = (bf16[256,128]{1,0:T(8,128)(2,1)S(1)}, bf16[256,128]{1,0:T(8,128)(2,1)S(1)}, u32[]{:S(2)}, u32[]{:S(2)}) collective-permute-start(bf16[256,128]{1,0:T(8,128)(2,1)S(1)} %fusion.47), channel_id=1, source_target_pairs={{16,0},{32,16},{48,32},{64,48},{80,64},{96,80},{112,96},{128,112},... | collective-permute-start | bytes 196616 | tf_op jit(solution)/shard_map/ppermute | solution.py:23
  302.9 6.2 %collective-permute-start.6 = (bf16[256,128]{1,0:T(8,128)(2,1)S(1)}, bf16[256,128]{1,0:T(8,128)(2,1)S(1)}, u32[]{:S(2)}, u32[]{:S(2)}) collective-permute-start(bf16[256,128]{1,0:T(8,128)(2,1)S(1)} %fusion.47), channel_id=1, source_target_pairs={{0,16},{16,32},{32,48},{48,64},{64,80},{80,96},{96,112},{112,128},... | collective-permute-start | bytes 196616 | tf_op jit(solution)/shard_map/ppermute | solution.py:22
  361.5 6.9 %collective-permute-start.8 = (f32[256,128]{1,0:T(8,128)S(1)}, f32[256,128]{1,0:T(8,128)S(1)}, u32[]{:S(2)}, u32[]{:S(2)}) collective-permute-start(f32[256,128]{1,0:T(8,128)S(1)} %get-tuple-element.11), channel_id=1, source_target_pairs={{16,0},{32,16},{48,32},{64,48},{80,64},{96,80},{112,96},{128,112},... | collective-permute-start | bytes 393224 | tf_op jit(solution)/shard_map/ppermute | solution.py:12
  363.4 6.9 %collective-permute-start.9 = (f32[256,128]{1,0:T(8,128)S(1)}, f32[256,128]{1,0:T(8,128)S(1)}, u32[]{:S(2)}, u32[]{:S(2)}) collective-permute-start(f32[256,128]{1,0:T(8,128)S(1)} %get-tuple-element.12), channel_id=1, source_target_pairs={{0,16},{16,32},{32,48},{48,64},{64,80},{80,96},{96,112},{112,128},... | collective-permute-start | bytes 393224 | tf_op jit(solution)/shard_map/ppermute | solution.py:12
where the time goes:
time: 477 us; the launch traced here: 476 us
  blocking collectives  399 us (84%)
  starting transfers between devices  29.4 us (6%)
  other arithmetic  24.3 us (5%)
  waiting for transfers between devices  14.6 us (3%)
    psum x1, blocking collectives, on_device(): norm_now = lax.psum(column_sums(residual, residual), ('span', 'sub'))  108 us
    psum x1, blocking collectives, on_device(): curve = lax.psum(column_sums(direction, image), ('span', 'sub'))  105 us
    psum x1, blocking collectives, on_device(): norm_next = lax.psum(column_sums(residual, residual), ('span', 'sub'))  94.5 us
    psum x2, blocking collectives, on_device(): lax.psum(corner_part.astype(jnp.bfloat16), 'sub').astype(jnp.float32)  91.4 us
    scatter-add x3, other arithmetic, assemble(): jnp.zeros((3 * owned, loads), jnp.float32).at[window_pos]  19.1 us
    ppermute x6, starting transfers between devices, from_behind(): return lax.ppermute(shard, axis, pairs)  17.5 us
  transfers between devices with their start and end apart: 10, of which 10 were waited for; matrix products, arithmetic and copies ran while one was open for 0% of the time, Pallas kernels for 0%

commit v1 on v0

--- a/solution.py
+++ b/solution.py
@@ -2,8 +2,14 @@
 import jax.numpy as jnp
 from jax import lax
 from jax.sharding import PartitionSpec as P
+from jax.lax import all_gather
 
 ITERS = 2
+
+
+def reach_numbers(x_part, a_name):
+    x_now = all_gather(x_part, a_name).sum(axis=0)
+    return x_now
 
 
 def from_behind(shard, axis, by):
@@ -85,7 +91,7 @@
         corner_part = jnp.einsum(
             "smc,smr->cr", corner_map, gathered, preferred_element_type=jnp.float32
         )
-        corner_residual = lax.psum(corner_part.astype(jnp.bfloat16), "sub").astype(jnp.float32)
+        corner_residual = reach_numbers(corner_part.astype(jnp.bfloat16), "sub").astype(jnp.float32)
         corner_update = jnp.dot(kernel, corner_residual, precision=lax.Precision.HIGHEST)
         spread_corners = jnp.einsum(
             "smc,cr->smr",

time: 477 us -> 431 us (0.904)
  the two profiles are of different devices: /device:TPU:10 before, /device:TPU:1 now
where the time goes in v1:
time: 431 us
  blocking collectives  357 us (83%)
  starting transfers between devices  25.8 us (6%)
  other arithmetic  24.9 us (6%)
  waiting for transfers between devices  14.1 us (3%)
  local copies, waits for them, and re-layouts  4.37 us (1%)
    psum x1, blocking collectives, on_device(): norm_now = lax.psum(column_sums(residual, residual), ('span', 'sub'))  112 us
    psum x1, blocking collectives, on_device(): curve = lax.psum(column_sums(direction, image), ('span', 'sub'))  106 us
    psum x1, blocking collectives, on_device(): norm_next = lax.psum(column_sums(residual, residual), ('span', 'sub'))  94.4 us
    all_gather x2, blocking collectives, reach_numbers(): x_now = all_gather(x_part, a_name).sum(axis=0)  44.6 us
    scatter-add x3, other arithmetic, assemble(): jnp.zeros((3 * owned, loads), jnp.float32).at[window_pos]  19.1 us
    ppermute x6, starting transfers between devices, from_behind(): return lax.ppermute(shard, axis, pairs)  16.4 us
  transfers between devices with their start and end apart: 10, of which 8 were waited for; matrix products, arithmetic and copies ran while one was open for 0% of the time, Pallas kernels for 0%

profile of v1, /device:TPU:1, one launch (start us, length us, event | category | flops | bytes accessed | tf_op | source)
XLA Modules:
  0.0 430.6 jit_solution(13277407826748545491)
XLA Ops:
  3.4 1.3 fusion.46
  5.6 6.9 %scatter_custom_fusion = f32[768,128]{1,0:T(8,128)S(1)} fusion(s32[768]{0:T(1024)S(1)} %fusion.43, bf16[1,768,128]{2,1,0:T(8,128)(2,1)} %param.10, f32[768]{0:T(1024)S(1)} %fusion.41, f32[768]{0:T(1024)S(1)} %multiply_reduce_fusion.4, f32[768]{0:T(1024)S(1)} %fusion.46, f32[]{:T(128)} %constant.47.clone.1), kind=kCustom, calls=%fused_computation.27 | custom fusion | flops 491520 | bytes 602116 | tf_op jit(solution)/shard_map/scatter-add | solution.py:69
  12.5 1.3 collective-permute-start
  13.8 4.6 %collective-permute-start.1 = (f32[256,128]{1,0:T(8,128)S(1)}, f32[256,128]{1,0:T(8,128)S(1)}, u32[]{:S(2)}, u32[]{:S(2)}) collective-permute-start(f32[256,128]{1,0:T(8,128)S(1)} %get-tuple-element.16), channel_id=1, source_target_pairs={{0,16},{16,32},{32,48},{48,64},{64,80},{80,96},{96,112},{112,128},... | collective-permute-start | bytes 393224 | tf_op jit(solution)/shard_map/ppermute | solution.py:18
  18.8 1.5 collective-permute-done.1
  20.4 3.9 collective-permute-start.2
  24.3 1.3 collective-permute-start.3
  25.6 3.7 collective-permute-done.3
  29.3 1.9 gather_fusion
  31.6 24.7 %all-gather = bf16[2048,128]{0,1:T(8,128)(2,1)S(1)} all-gather(bf16[128,128]{0,1:T(8,128)(2,1)S(1)} %fusion.8), channel_id=2, replica_groups=mesh['span'=32,'sub'=16] {'sub'}, dimensions={0}, use_global_device_ids=true | all-gather | bytes 557056 | tf_op jit(solution)/shard_map/all_gather | solution.py:11
  58.0 6.1 %scatter_custom_fusion.1 = f32[768,128]{1,0:T(8,128)S(1)} fusion(s32[768]{0:T(1024)S(1)} %fusion.43, f32[768,128]{1,0:T(8,128)S(1)} %copy.16, f32[]{:T(128)} %constant.47.clone.1), kind=kCustom, calls=%fused_computation.46 | custom fusion | flops 98304 | bytes 393220 | tf_op jit(solution)/shard_map/scatter-add | solution.py:69
  64.1 1.3 collective-permute-start.4
  65.4 4.0 collective-permute-start.5
  69.4 1.5 collective-permute-done.4
  71.9 112.2 %all-reduce = (f32[128]{0:T(128)S(1)}, f32[128]{0:T(128)S(1)}) all-reduce(f32[128]{0:T(128)S(1)} %get-tuple-element.3, f32[128]{0:T(128)S(1)} %get-tuple-element.2), channel_id=1, replica_groups=mesh['span'=32,'sub'=16] {'span','sub'}, use_global_device_ids=true, to_apply=%region_4.5 | all-reduce | flops 256 | bytes 2048 | tf_op jit(solution)/shard_map/psum | solution.py:80
  184.1 94.4 %psum.30 = f32[128]{0:T(128)S(1)} all-reduce(f32[128]{0:T(128)S(1)} %multiply_reduce_fusion.1), channel_id=1, replica_groups=mesh['span'=32,'sub'=16] {'span','sub'}, use_global_device_ids=true, to_apply=%region_10.11 | all-reduce | flops 128 | bytes 1024 | tf_op jit(solution)/shard_map/psum | solution.py:107
  278.6 2.8 collective-permute-start.6
  282.7 3.7 collective-permute-done.7
  286.5 1.9 gather_fusion.1
  289.4 19.9 %all-gather.1 = bf16[2048,128]{0,1:T(8,128)(2,1)S(1)} all-gather(bf16[128,128]{0,1:T(8,128)(2,1)S(1)} %fusion.9), channel_id=3, replica_groups=mesh['span'=32,'sub'=16] {'sub'}, dimensions={0}, use_global_device_ids=true | all-gather | bytes 557056 | tf_op jit(solution)/shard_map/all_gather | solution.py:11
  310.3 6.1 %scatter_custom_fusion.2 = f32[768,128]{1,0:T(8,128)S(1)} fusion(s32[768]{0:T(1024)S(1)} %fusion.43, f32[768,128]{1,0:T(8,128)S(1)} %copy.17, f32[]{:T(128)} %constant.47.clone.1), kind=kCustom, calls=%fused_computation.44 | custom fusion | flops 98304 | bytes 393220 | tf_op jit(solution)/shard_map/scatter-add | solution.py:69
  317.8 4.0 collective-permute-start.9
  321.8 1.5 collective-permute-done.8
  324.2 105.6 %psum.31 = f32[128]{0:T(128)S(1)} all-reduce(f32[128]{0:T(128)S(1)} %multiply_reduce_fusion), channel_id=1, replica_groups=mesh['span'=32,'sub'=16] {'span','sub'}, use_global_device_ids=true, to_apply=%region_14.15 | all-reduce | flops 128 | bytes 1024 | tf_op jit(solution)/shard_map/psum | solution.py:103
  (46 shorter events, 12.6 us)
Async XLA Ops:
  0.6 56.1 %copy-start = (bf16[1,768,768]{2,1,0:T(8,128)(2,1)S(1)}, bf16[1,768,768]{2,1,0:T(8,128)(2,1)}, u32[]{:S(2)}) copy-start(bf16[1,768,768]{2,1,0:T(8,128)(2,1)} %param.17) | copy-start | bytes 3538948
  12.5 6.3 %collective-permute-start = (f32[256,128]{1,0:T(8,128)S(1)}, f32[256,128]{1,0:T(8,128)S(1)}, u32[]{:S(2)}, u32[]{:S(2)}) collective-permute-start(f32[256,128]{1,0:T(8,128)S(1)} %get-tuple-element.15), channel_id=1, source_target_pairs={{16,0},{32,16},{48,32},{64,48},{80,64},{96,80},{112,96},{128,112},... | collective-permute-start | bytes 393224 | tf_op jit(solution)/shard_map/ppermute | solution.py:18
  13.8 6.5 %collective-permute-start.1 = (f32[256,128]{1,0:T(8,128)S(1)}, f32[256,128]{1,0:T(8,128)S(1)}, u32[]{:S(2)}, u32[]{:S(2)}) collective-permute-start(f32[256,128]{1,0:T(8,128)S(1)} %get-tuple-element.16), channel_id=1, source_target_pairs={{0,16},{16,32},{32,48},{48,64},{64,80},{80,96},{96,112},{112,128},... | collective-permute-start | bytes 393224 | tf_op jit(solution)/shard_map/ppermute | solution.py:18
  20.4 10.8 %copy-start.1 = (bf16[1,768,128]{2,1,0:T(8,128)(2,1)S(1)}, bf16[1,768,128]{2,1,0:T(8,128)(2,1)}, u32[]{:S(2)}) copy-start(bf16[1,768,128]{2,1,0:T(8,128)(2,1)} %param.18) | copy-start | bytes 589828
  20.4 5.2 %collective-permute-start.2 = (bf16[256,128]{1,0:T(8,128)(2,1)S(1)}, bf16[256,128]{1,0:T(8,128)(2,1)S(1)}, u32[]{:S(2)}, u32[]{:S(2)}) collective-permute-start(bf16[256,128]{1,0:T(8,128)(2,1)S(1)} %get-tuple-element.7), channel_id=1, source_target_pairs={{0,16},{16,32},{32,48},{48,64},{64,80},{80,96},{96,112},{112,128},... | collective-permute-start | bytes 196616 | tf_op jit(solution)/shard_map/ppermute | solution.py:28
  24.3 5.0 %collective-permute-start.3 = (bf16[256,128]{1,0:T(8,128)(2,1)S(1)}, bf16[256,128]{1,0:T(8,128)(2,1)S(1)}, u32[]{:S(2)}, u32[]{:S(2)}) collective-permute-start(bf16[256,128]{1,0:T(8,128)(2,1)S(1)} %get-tuple-element.7), channel_id=1, source_target_pairs={{16,0},{32,16},{48,32},{64,48},{80,64},{96,80},{112,96},{128,112},... | collective-permute-start | bytes 196616 | tf_op jit(solution)/shard_map/ppermute | solution.py:29
  56.4 0.9 copy-start.2
  64.1 6.8 %collective-permute-start.4 = (f32[256,128]{1,0:T(8,128)S(1)}, f32[256,128]{1,0:T(8,128)S(1)}, u32[]{:S(2)}, u32[]{:S(2)}) collective-permute-start(f32[256,128]{1,0:T(8,128)S(1)} %get-tuple-element.13), channel_id=1, source_target_pairs={{16,0},{32,16},{48,32},{64,48},{80,64},{96,80},{112,96},{128,112},... | collective-permute-start | bytes 393224 | tf_op jit(solution)/shard_map/ppermute | solution.py:18
  65.4 6.4 %collective-permute-start.5 = (f32[256,128]{1,0:T(8,128)S(1)}, f32[256,128]{1,0:T(8,128)S(1)}, u32[]{:S(2)}, u32[]{:S(2)}) collective-permute-start(f32[256,128]{1,0:T(8,128)S(1)} %get-tuple-element.14), channel_id=1, source_target_pairs={{0,16},{16,32},{32,48},{48,64},{64,80},{80,96},{96,112},{112,128},... | collective-permute-start | bytes 393224 | tf_op jit(solution)/shard_map/ppermute | solution.py:18
  278.6 4.2 collective-permute-start.6
  281.4 5.0 %collective-permute-start.7 = (bf16[256,128]{1,0:T(8,128)(2,1)S(1)}, bf16[256,128]{1,0:T(8,128)(2,1)S(1)}, u32[]{:S(2)}, u32[]{:S(2)}) collective-permute-start(bf16[256,128]{1,0:T(8,128)(2,1)S(1)} %fusion.47), channel_id=1, source_target_pairs={{16,0},{32,16},{48,32},{64,48},{80,64},{96,80},{112,96},{128,112},... | collective-permute-start | bytes 196616 | tf_op jit(solution)/shard_map/ppermute | solution.py:29
  316.4 6.8 %collective-permute-start.8 = (f32[256,128]{1,0:T(8,128)S(1)}, f32[256,128]{1,0:T(8,128)S(1)}, u32[]{:S(2)}, u32[]{:S(2)}) collective-permute-start(f32[256,128]{1,0:T(8,128)S(1)} %get-tuple-element.11), channel_id=1, source_target_pairs={{16,0},{32,16},{48,32},{64,48},{80,64},{96,80},{112,96},{128,112},... | collective-permute-start | bytes 393224 | tf_op jit(solution)/shard_map/ppermute | solution.py:18
  317.8 6.4 %collective-permute-start.9 = (f32[256,128]{1,0:T(8,128)S(1)}, f32[256,128]{1,0:T(8,128)S(1)}, u32[]{:S(2)}, u32[]{:S(2)}) collective-permute-start(f32[256,128]{1,0:T(8,128)S(1)} %get-tuple-element.12), channel_id=1, source_target_pairs={{0,16},{16,32},{32,48},{48,64},{64,80},{80,96},{96,112},{112,128},... | collective-permute-start | bytes 393224 | tf_op jit(solution)/shard_map/ppermute | solution.py:18
